TPU v7x, 32 devices: a whole 2x2x4 slice. The times are simulated.
32 devices in a mesh: seq: 8 (over z, y), head: 4 (over x, core).
Axes of the slice: x: 2, y: 2, z: 4, core: 2. Of those that a mesh axis runs over, the one named last changes fastest.
Arguments:
- residual: bfloat16 [1024, 8192], P('seq', 'head'), may hold values from -45 to 45
- key_gate: bfloat16 [1024, 8192], P('seq', 'head'), may hold values from -6 to 6
- query_gate: bfloat16 [1024, 8192], P('seq', 'head'), may hold values from -6 to 6
- norm_gain: float32 [8192], P('head'), may hold values from 0.1 to 1.9
- filters: float32 [8192, 128], P('head'), may hold values from -0.5 to 0.5
- hyena_cotangent: bfloat16 [1024, 8192], P('seq', 'head'), may hold values from -6 to 6
- attn_query: bfloat16 [1024, 4096], P('seq', 'head'), may hold values from -6 to 6
- attention_keys: bfloat16 [1024, 512], P('seq', 'head'), may hold values from -6 to 6
- attention_values: bfloat16 [1024, 512], P('seq', 'head'), may hold values from -6 to 6
- attn_cotangent: bfloat16 [1024, 4096], P('seq', 'head'), may hold values from -6 to 6
- doc_ids: int32 [1024], P('seq'), may hold values from 0 to 3, never falling along the last dimension, each value on 1 to 768 neighbouring positions
Outputs:
- grad_residual: bfloat16 [1024, 8192], P('seq', 'head')
- grad_key_gate: bfloat16 [1024, 8192], P('seq', 'head')
- grad_query_gate: bfloat16 [1024, 8192], P('seq', 'head')
- grad_gain: float32 [8192], P('head')
- grad_filters: float32 [8192, 128], P('head')
- grad_query: bfloat16 [1024, 4096], P('seq', 'head')
- key_gradient: bfloat16 [1024, 512], P('seq', 'head')
- value_gradient: bfloat16 [1024, 512], P('seq', 'head')
Inputs may be any that keep to these rules, and one draw needn't show every extreme that they name: `doc_ids`: document ids never fall along the sequence; each document holds 1 to 768 tokens, and one holds exactly 768.
All inputs are finite; a program needn't handle non-finite values.
Results may differ from a plain program's by a relative error of at most 0.0076.
Values may be sent and summed in bfloat16 or wider, within the bound.
A program may use at most 64 MiB of HBM per device.

v0:
```python
from functools import partial

import jax
import jax.numpy as jnp
from jax import lax
from jax.sharding import PartitionSpec as P

D = 8192
HEAD_SIZE = 128


NORM_EPS = 1e-05
SCORE_FLOOR = -1e30


def shifted(block, axis, distance):
    devices = range(lax.axis_size(axis))
    route = [(i - distance, i) for i in devices if i - distance in devices]
    return lax.ppermute(block, axis, route)


def depthwise(signal, kernel):
    return lax.conv_general_dilated(
        signal[None],
        kernel[:, None, :],
        (1,),
        ((0, 0),),
        dimension_numbers=("NWC", "WIO", "NWC"),
        feature_group_count=signal.shape[1],
        precision=lax.Precision.HIGHEST,
    )[0]


def on_device(
    residual,
    key_gate,
    query_gate,
    norm_gain,
    filters,
    hyena_cotangent,
    attn_query,
    attention_keys,
    attention_values,
    attn_cotangent,
    doc_ids,
):
    local_rows, channels = residual.shape
    rim_width = filters.shape[1] - 1
    signal_rows = residual.astype(jnp.float32)
    gates_k = key_gate.astype(jnp.float32)
    squares = lax.psum(jnp.sum(signal_rows * signal_rows, axis=1), "head")
    inverse = lax.rsqrt(squares[:, None] / D + NORM_EPS)
    gated_rows = (signal_rows * inverse * norm_gain * gates_k).astype(jnp.bfloat16)
    earlier = shifted(gated_rows[local_rows - rim_width :], "seq", 1)
    gated_wide = jnp.concatenate([earlier, gated_rows], 0)
    normed = signal_rows * inverse
    scaled = normed * norm_gain
    gated_f = lax.optimization_barrier(gated_wide).astype(jnp.float32)
    filtered = depthwise(gated_f, jnp.flip(filters, 1).T)
    upstream = hyena_cotangent.astype(jnp.float32)
    grad_query_gate = (upstream * filtered).astype(jnp.bfloat16)
    inner_grad = (upstream * query_gate.astype(jnp.float32)).astype(jnp.bfloat16)
    later_rows = shifted(inner_grad[:rim_width], "seq", -1)
    inner_f = lax.optimization_barrier(jnp.concatenate([inner_grad, later_rows], 0)).astype(
        jnp.float32
    )
    back_conv = depthwise(inner_f, filters.T)
    grad_key_gate = (back_conv * scaled).astype(jnp.bfloat16)
    grad_scaled = back_conv * gates_k
    part_gain = jnp.sum(grad_scaled * normed, axis=0)
    along_rows = lax.psum(jnp.sum(norm_gain * grad_scaled * normed, axis=1), "head")
    grad_residual = (inverse * (norm_gain * grad_scaled - normed * along_rows[:, None] / D)).astype(
        jnp.bfloat16
    )
    tap_sums = depthwise(gated_f, inner_f[:local_rows])
    part_filters = jnp.flip(tap_sums, 0).T
    grad_filters, grad_gain = lax.psum((part_filters, part_gain), "seq")
    score_scale = HEAD_SIZE ** (-0.5)
    my_index = lax.axis_index("seq")
    key_all, value_all, docs_wire = (
        lax.all_gather(attention_keys, "seq", axis=0, tiled=True),
        lax.all_gather(attention_values, "seq", axis=0, tiled=True),
        lax.all_gather(doc_ids.astype(jnp.bfloat16), "seq", axis=0, tiled=True),
    )
    docs_all = docs_wire.astype(jnp.int32)
    total_rows = key_all.shape[0]
    block_rows = min(512, total_rows)
    head_count = attn_query.shape[1] // HEAD_SIZE
    kv_width = attention_keys.shape[1]
    half_rows = local_rows // 2
    offsets = jnp.arange(half_rows, dtype=jnp.int32)
    first_start = my_index * local_rows

    def make_mask(positions, doc_rows, key_start, span_rows):
        key_pos = key_start + jnp.arange(span_rows, dtype=jnp.int32)
        key_docs = lax.dynamic_slice_in_dim(docs_all, key_start, span_rows)
        allowed = (key_pos[None, :] <= positions[:, None]) & (
            key_docs[None, :] == doc_rows[:, None]
        )
        return jnp.broadcast_to(allowed[:, None, :], (half_rows, head_count, span_rows)).reshape(
            half_rows * head_count, span_rows
        )

    def needed(positions, doc_rows, key_start, span_rows):
        last_doc = lax.dynamic_index_in_dim(docs_all, key_start + span_rows - 1, keepdims=False)
        return (key_start <= positions[half_rows - 1]) & (last_doc >= doc_rows[0])

    def group_stats(query_flat, cotangent_flat, positions, doc_rows):
        flat_rows = query_flat.shape[0]

        def group_update(key_start, state_now):
            top_old, total_old, weighted_old = state_now
            key_blk = lax.dynamic_slice_in_dim(key_all, key_start, block_rows, 0)
            value_blk = lax.dynamic_slice_in_dim(value_all, key_start, block_rows, 0)
            allowed = make_mask(positions, doc_rows, key_start, block_rows)
            scores = (
                jnp.einsum("rd,kd->rk", query_flat, key_blk, preferred_element_type=jnp.float32)
                * score_scale
            )
            scores = jnp.where(allowed, scores, SCORE_FLOOR)
            top_new = jnp.maximum(top_old, jnp.max(scores, axis=1))
            fade_factor = jnp.exp(top_old - top_new)
            prob_block = jnp.where(allowed, jnp.exp(scores - top_new[:, None]), 0.0)
            dprobs = jnp.einsum(
                "rd,kd->rk", cotangent_flat, value_blk, preferred_element_type=jnp.float32
            )
            return (
                top_new,
                total_old * fade_factor + jnp.sum(prob_block, axis=1),
                weighted_old * fade_factor + jnp.sum(prob_block * dprobs, axis=1),
            )

        def group_advance(number, state_now):
            key_start = number * block_rows
            return lax.cond(
                needed(positions, doc_rows, key_start, block_rows),
                partial(group_update, key_start),
                lambda state_same: state_same,
                state_now,
            )

        initial = (
            jnp.full((flat_rows,), SCORE_FLOOR, jnp.float32),
            jnp.zeros((flat_rows,), jnp.float32),
            jnp.zeros((flat_rows,), jnp.float32),
        )
        top_row, total_row, weighted_row = lax.fori_loop(
            0, total_rows // block_rows, group_advance, initial
        )
        return (top_row + jnp.log(total_row), weighted_row / total_row)

    def prepare(queries, cotangent, row_start):
        query_flat = queries.reshape(half_rows * head_count, HEAD_SIZE)
        cotangent_flat = cotangent.reshape(half_rows * head_count, HEAD_SIZE)
        positions = row_start + offsets
        doc_rows = lax.dynamic_slice_in_dim(docs_all, row_start, half_rows)
        log_total, row_delta = group_stats(query_flat, cotangent_flat, positions, doc_rows)
        return (query_flat, cotangent_flat, positions, doc_rows, log_total, row_delta)

    def block_terms(group, key_start, span_rows):
        query_flat, cotangent_flat, positions, doc_rows, log_total, row_delta = group
        key_blk = lax.dynamic_slice_in_dim(key_all, key_start, span_rows, 0)
        value_blk = lax.dynamic_slice_in_dim(value_all, key_start, span_rows, 0)
        allowed = make_mask(positions, doc_rows, key_start, span_rows)
        scores = (
            jnp.einsum("rd,kd->rk", query_flat, key_blk, preferred_element_type=jnp.float32)
            * score_scale
        )
        prob_block = jnp.where(allowed, jnp.exp(scores - log_total[:, None]), 0.0)
        dprobs = jnp.einsum(
            "rd,kd->rk", cotangent_flat, value_blk, preferred_element_type=jnp.float32
        )
        dscores = (prob_block * (dprobs - row_delta[:, None])).astype(jnp.bfloat16)
        return (key_blk, prob_block, dscores)

    def key_value_terms(group, prob_block, dscores):
        grad_k = (
            jnp.einsum("rk,rd->kd", dscores, group[0], preferred_element_type=jnp.float32)
            * score_scale
        )
        grad_v = jnp.einsum(
            "rk,rd->kd",
            prob_block.astype(jnp.bfloat16),
            group[1],
            preferred_element_type=jnp.float32,
        )
        return jnp.concatenate([grad_k, grad_v], axis=1)

    second = (attn_query[half_rows:], attn_cotangent[half_rows:], first_start + half_rows)
    groups = [
        prepare(attn_query[:half_rows], attn_cotangent[:half_rows], first_start),
        prepare(second[0], second[1], second[2]),
    ]
    flat_rows = half_rows * head_count

    def full_sweep(group, buffer_in):

        def full_update(key_start, state_now):
            grad_rows, buffer_now = state_now
            key_blk, prob_block, dscores = block_terms(group, key_start, block_rows)
            grad_rows = (
                grad_rows
                + jnp.einsum("rk,kd->rd", dscores, key_blk, preferred_element_type=jnp.float32)
                * score_scale
            )
            new_terms = key_value_terms(group, prob_block, dscores)
            current = lax.dynamic_slice_in_dim(buffer_now, key_start, block_rows, 0)
            return (
                grad_rows,
                lax.dynamic_update_slice_in_dim(buffer_now, current + new_terms, key_start, 0),
            )

        def full_advance(number, state_now):
            key_start = number * block_rows
            return lax.cond(
                needed(group[2], group[3], key_start, block_rows),
                partial(full_update, key_start),
                lambda state_same: state_same,
                state_now,
            )

        return lax.fori_loop(
            0,
            total_rows // block_rows,
            full_advance,
            (jnp.zeros((flat_rows, HEAD_SIZE), jnp.float32), buffer_in),
        )

    buffer_all = jnp.zeros((total_rows, 2 * kv_width), jnp.float32)
    grads_first, buffer_all = full_sweep(groups[0], buffer_all)
    grads_second, buffer_all = full_sweep(groups[1], buffer_all)
    key_terms = lax.psum_scatter(buffer_all, "seq", scatter_dimension=0, tiled=True)
    first_low = grads_first.astype(jnp.bfloat16).reshape(half_rows, head_count * HEAD_SIZE)
    second_low = grads_second.astype(jnp.bfloat16).reshape(half_rows, head_count * HEAD_SIZE)
    grad_query = jnp.concatenate([first_low, second_low], axis=0)
    key_gradient = key_terms[:, :kv_width].astype(jnp.bfloat16)
    value_gradient = key_terms[:, kv_width:].astype(jnp.bfloat16)
    return (
        grad_residual,
        grad_key_gate,
        grad_query_gate,
        grad_gain,
        grad_filters,
        grad_query,
        key_gradient,
        value_gradient,
    )


def solution(mesh):
    return jax.shard_map(
        on_device,
        mesh=mesh,
        in_specs=(
            P("seq", "head"),
            P("seq", "head"),
            P("seq", "head"),
            P("head"),
            P("head", None),
            P("seq", "head"),
            P("seq", "head"),
            P("seq", "head"),
            P("seq", "head"),
            P("seq", "head"),
            P("seq"),
        ),
        out_specs=(
            P("seq", "head"),
            P("seq", "head"),
            P("seq", "head"),
            P("head"),
            P("head", None),
            P("seq", "head"),
            P("seq", "head"),
            P("seq", "head"),
        ),
        check_vma=False,
    )
```

profile of v0, /device:TPU:26, one launch (start us, length us, event | category | flops | bytes accessed | tf_op | source)
XLA Modules:
  0.0 269.0 jit_solution(12140785390327315428)
XLA Ops:
  7.2 1.4 fusion.71
  8.7 3.3 %collective-permute-start = (bf16[127,2048]{1,0:T(8,128)(2,1)S(1)}, bf16[127,2048]{1,0:T(8,128)(2,1)S(1)}, u32[]{:S(2)}, u32[]{:S(2)}) collective-permute-start(bf16[127,2048]{1,0:T(8,128)(2,1)S(1)} %bitcast.136), channel_id=1, source_target_pairs={{4,0},{8,4},{12,8},{16,12},{20,16},{24,20},{28,24},{5,1},{9,5},{13... | collective-permute-start | bytes 1560584 | tf_op jit(solution)/shard_map/ppermute | solution.py:19
  12.2 1.9 copy.58
  14.1 5.9 %psum.28 = f32[128]{0:T(128)S(1)} all-reduce(f32[128]{0:T(128)S(1)} %fusion.70), channel_id=1, replica_groups=mesh['seq'=8,'head'=4] {'head'}, use_global_device_ids=true, to_apply=%region_1.0 | all-reduce | flops 128 | bytes 1024 | tf_op jit(solution)/shard_map/psum | solution.py:51
  20.1 4.1 %collective-permute-done = bf16[127,2048]{1,0:T(8,128)(2,1)S(1)} collective-permute-done((bf16[127,2048]{1,0:T(8,128)(2,1)S(1)}, bf16[127,2048]{1,0:T(8,128)(2,1)S(1)}, u32[]{:S(2)}, u32[]{:S(2)}) %collective-permute-start) | collective-permute-done | bytes 520224 | tf_op jit(solution)/shard_map/ppermute | solution.py:19
  24.4 11.4 %fusion.52 = f32[1,128,2048]{2,0,1:T(1,128)S(1)} fusion(f32[128,1,2048]{2,1,0:T(1,128)S(1)} %copy-done.9, bf16[1,255,2048]{2,1,0:T(8,128)(2,1)S(1)} %bitcast.135), kind=kOutput, calls=%fused_computation.86 | convolution fusion | flops 402653184 | bytes 3141632 | tf_op jit(solution)/shard_map/conv_general_dilated | solution.py:23
  36.4 5.9 %psum.29 = f32[128]{0:T(128)S(1)} all-reduce(f32[128]{0:T(128)S(1)} %get-tuple-element.1731), channel_id=1, replica_groups=mesh['seq'=8,'head'=4] {'head'}, use_global_device_ids=true, to_apply=%region_3.4 | all-reduce | flops 128 | bytes 1024 | tf_op jit(solution)/shard_map/psum | solution.py:71
  42.3 1.7 fusion.63
  44.1 2.1 collective-permute-start.1
  46.2 0.7 fusion.77
  46.9 13.6 %collective-permute-done.1 = bf16[127,2048]{1,0:T(8,128)(2,1)S(1)} collective-permute-done((bf16[127,2048]{1,0:T(8,128)(2,1)S(1)}, bf16[127,2048]{1,0:T(8,128)(2,1)S(1)}, u32[]{:S(2)}, u32[]{:S(2)}) %collective-permute-start.1) | collective-permute-done | bytes 520224 | tf_op jit(solution)/shard_map/ppermute | solution.py:19
  60.7 14.9 %fusion.54 = f32[1,128,2048]{2,0,1:T(1,128)S(1)} fusion(bf16[1,255,2048]{2,1,0:T(8,128)(2,1)S(1)} %bitcast.137, bf16[128,1,2048]{2,0,1:T(8,128)(2,1)S(1)} %slice_bitcast_fusion), kind=kOutput, calls=%fused_computation.88 | convolution fusion | flops 67108864 | bytes 2617344 | tf_op jit(solution)/shard_map/conv_general_dilated | solution.py:23
  75.9 5.3 %rev.9 = f32[128,2048]{1,0:T(8,128)} reverse(f32[128,2048]{1,0:T(8,128)S(1)} %bitcast.134), dimensions={0} | reverse | bytes 2097152 | tf_op jit(solution)/shard_map/jit(_flip)/rev | solution.py:76
  81.8 14.0 %all-gather = bf16[8,1,128]{2,1,0:T(2,128)(2,1)S(1)} all-gather(bf16[1,1,128]{2,1,0:T(2,128)(2,1)S(1)} %convert_bitcast_fusion), channel_id=1, replica_groups=mesh['seq'=8,'head'=4] {'seq'}, dimensions={0}, use_global_device_ids=true | all-gather | bytes 2304 | tf_op jit(solution)/shard_map/all_gather | solution.py:83
  96.2 32.9 %all_gather.10 = bf16[1024,128]{1,0:T(8,128)(2,1)S(1)} all-gather(bf16[128,128]{1,0:T(8,128)(2,1)S(1)} %copy-done.14), channel_id=1, replica_groups=mesh['seq'=8,'head'=4] {'seq'}, dimensions={0}, use_global_device_ids=true | all-gather | bytes 294912 | tf_op jit(solution)/shard_map/all_gather | solution.py:81
  129.0 31.3 %all_gather.11 = bf16[1024,128]{1,0:T(8,128)(2,1)S(1)} all-gather(bf16[128,128]{1,0:T(8,128)(2,1)S(1)} %copy-done.15), channel_id=1, replica_groups=mesh['seq'=8,'head'=4] {'seq'}, dimensions={0}, use_global_device_ids=true | all-gather | bytes 294912 | tf_op jit(solution)/shard_map/all_gather | solution.py:82
  160.4 8.0 %while.80 = (s32[]{:T(128)}, f32[512]{0:T(512)S(1)}, f32[512]{0:T(512)S(1)}, f32[512]{0:T(512)S(1)}, s32[64]{0:T(128)S(1)}, /*index=5*/s32[1024]{0:T(1024)S(1)},...) while((s32[]{:T(128)}, f32[512]{0:T(512)S(1)}, ...), condition=%wide.region_13.14_spmd, body=%wide.region_7.13_spmd.sunk | while | flops 136939536 | bytes 5356479 | solution.py:147
  162.6 1.8 conditional.8
  166.6 1.8 conditional.8
  168.5 10.0 %while.81 = (s32[]{:T(128)}, f32[512,128]{1,0:T(8,128)S(1)}, f32[1024,256]{1,0:T(8,128)S(1)}, s32[64]{0:T(128)S(1)}, s32[1024]{0:T(1024)S(1)}, /*index=5*/s32[64...) while((s32[]{:T(128)}, f32[512,128]{1,0:T(8,128)S(1)}, ...), condition=%wide.region_17.18_spmd, body=%wide.region_14.17_spmd.sunk | while | flops 337936896 | bytes 9386951 | solution.py:222
  168.5 0.6 dynamic_slice.136
  169.8 0.6 slice.159
  171.0 2.5 conditional.9
  173.5 0.6 dynamic_slice.136
  174.8 0.6 slice.159
  176.0 2.5 conditional.9
  178.6 8.6 %while.82 = (s32[]{:T(128)}, f32[512]{0:T(512)S(1)}, f32[512]{0:T(512)S(1)}, f32[512]{0:T(512)S(1)}, s32[64]{0:T(128)S(1)}, /*index=5*/s32[1024]{0:T(1024)S(1)},...) while((s32[]{:T(128)}, f32[512]{0:T(512)S(1)}, ...), condition=%wide.region_24.25_spmd, body=%wide.region_18.24_spmd.sunk | while | flops 136939536 | bytes 5356479 | solution.py:147
  178.6 0.6 dynamic_slice.137
  179.8 0.6 slice.160
  181.1 1.8 conditional.10
  182.9 0.6 dynamic_slice.137
  185.3 1.8 conditional.10
  187.2 10.0 %while.83 = (s32[]{:T(128)}, f32[512,128]{1,0:T(8,128)S(1)}, f32[1024,256]{1,0:T(8,128)S(1)}, s32[64]{0:T(128)S(1)}, s32[1024]{0:T(1024)S(1)}, /*index=5*/s32[64...) while((s32[]{:T(128)}, f32[512,128]{1,0:T(8,128)S(1)}, ...), condition=%wide.region_28.29_spmd, body=%wide.region_25.28_spmd.sunk | while | flops 337936896 | bytes 9386951 | solution.py:222
  187.2 0.6 dynamic_slice.138
  189.7 2.5 conditional.11
  192.2 0.6 dynamic_slice.138
  194.7 2.5 conditional.11
  197.2 1.0 copy-done
  198.2 1.4 rev.8
  199.8 0.8 copy.60
  200.6 0.7 pad_maximum_fusion.2
  201.3 15.1 %psum.30 = f32[2048]{0:T(1024)} all-reduce(f32[2048]{0:T(1024)S(1)} %get-tuple-element.1730), channel_id=1, replica_groups=mesh['seq'=8,'head'=4] {'seq'}, use_global_device_ids=true, to_apply=%region_5.6 | all-reduce | flops 2048 | bytes 16384 | tf_op jit(solution)/shard_map/psum | solution.py:77
  216.5 11.5 %fusion.56 = f32[1,128,2048]{2,0,1:T(1,128)S(1)} fusion(f32[128,1,2048]{2,1,0:T(1,128)S(1)} %copy.60, bf16[1,255,2048]{2,1,0:T(8,128)(2,1)S(1)} %bitcast.138), kind=kOutput, calls=%fused_computation.90 | convolution fusion | flops 402653184 | bytes 3141632 | tf_op jit(solution)/shard_map/conv_general_dilated | solution.py:23
  228.0 1.1 fusion.72
  229.1 2.5 copy.63
  231.6 28.9 %reduce-scatter.2.cloned.1.call-done = f32[128,256]{1,0:T(8,128)} async-done(((f32[1024,256]{1,0:T(8,128)}), f32[128,256]{1,0:T(8,128)}) %reduce-scatter.2.cloned.1.call-update) | async-done | bytes 131088 | tf_op jit(solution)/shard_map/reduce_scatter | solution.py:232
  260.6 0.9 convert.4
  261.5 0.6 fusion.79
  (166 shorter events, 23.2 us)
Async XLA Ops:
  7.2 4.8 %copy-start.1 = (bf16[128,2048]{1,0:T(8,128)(2,1)S(1)}, bf16[128,2048]{1,0:T(8,128)(2,1)}, u32[]{:S(2)}) copy-start(bf16[128,2048]{1,0:T(8,128)(2,1)} %param.27) | copy-start | bytes 1572868
  7.2 5.0 %copy-start.2 = (f32[2048,128]{1,0:T(8,128)S(1)}, f32[2048,128]{1,0:T(8,128)}, u32[]{:S(2)}) copy-start(f32[2048,128]{1,0:T(8,128)} %param.31) | copy-start | bytes 3145732
  7.2 221.9 %all-reduce.2.cloned.1.call-start = ((), (), s32[]{:S(2)}) async-start(), calls=%async_computation.1 | async-start | bytes 2097152 | tf_op jit(solution)/shard_map/psum | solution.py:77
  8.7 15.6 %collective-permute-start = (bf16[127,2048]{1,0:T(8,128)(2,1)S(1)}, bf16[127,2048]{1,0:T(8,128)(2,1)S(1)}, u32[]{:S(2)}, u32[]{:S(2)}) collective-permute-start(bf16[127,2048]{1,0:T(8,128)(2,1)S(1)} %bitcast.136), channel_id=1, source_target_pairs={{4,0},{8,4},{12,8},{16,12},{20,16},{24,20},{28,24},{5,1},{9,5},{13... | collective-permute-start | bytes 1560584 | tf_op jit(solution)/shard_map/ppermute | solution.py:19
  12.2 7.8 %copy-start.11 = (bf16[128,1024]{1,0:T(8,128)(2,1)S(1)}, bf16[128,1024]{1,0:T(8,128)(2,1)}, u32[]{:S(2)}) copy-start(bf16[128,1024]{1,0:T(8,128)(2,1)} %param.33) | copy-start | bytes 786436
  20.1 4.2 %copy-start.9 = (f32[128,1,2048]{2,1,0:T(1,128)S(1)}, f32[128,1,2048]{2,1,0:T(1,128)}, u32[]{:S(2)}) copy-start(f32[128,1,2048]{2,1,0:T(1,128)} %copy.58) | copy-start | bytes 3145732
  24.3 11.5 %copy-start.3 = (bf16[255,2048]{1,0:T(8,128)(2,1)}, bf16[255,2048]{1,0:T(8,128)(2,1)S(1)}, u32[]{:S(2)}) copy-start(bf16[255,2048]{1,0:T(8,128)(2,1)S(1)} %pad_maximum_fusion) | copy-start | bytes 3133444
  24.3 11.5 %copy-start.6 = (bf16[128,2048]{1,0:T(8,128)(2,1)S(1)}, bf16[128,2048]{1,0:T(8,128)(2,1)}, u32[]{:S(2)}) copy-start(bf16[128,2048]{1,0:T(8,128)(2,1)} %param.28) | copy-start | bytes 1572868
  24.3 11.5 %copy-start.13 = (f32[2048]{0:T(1024)S(1)}, f32[2048]{0:T(1024)}, u32[]{:S(2)}) copy-start(f32[2048]{0:T(1024)} %param.30) | copy-start | bytes 24580
  42.3 3.9 %copy-start.12 = (bf16[128,1024]{1,0:T(8,128)(2,1)S(1)}, bf16[128,1024]{1,0:T(8,128)(2,1)}, u32[]{:S(2)}) copy-start(bf16[128,1024]{1,0:T(8,128)(2,1)} %param.36) | copy-start | bytes 786436
  44.0 2.9 %copy-start.4 = (bf16[255,2048]{1,0:T(8,128)(2,1)S(1)}, bf16[255,2048]{1,0:T(8,128)(2,1)}, u32[]{:S(2)}) copy-start(bf16[255,2048]{1,0:T(8,128)(2,1)} %copy-done.3) | copy-start | bytes 3133444
  44.1 16.4 %collective-permute-start.1 = (bf16[127,2048]{1,0:T(8,128)(2,1)S(1)}, bf16[127,2048]{1,0:T(8,128)(2,1)S(1)}, u32[]{:S(2)}, u32[]{:S(2)}) collective-permute-start(bf16[127,2048]{1,0:T(8,128)(2,1)S(1)} %slice.143), channel_id=1, source_target_pairs={{0,4},{4,8},{8,12},{12,16},{16,20},{20,24},{24,28},{1,5},{5,9},{9,... | collective-permute-start | bytes 1560584 | tf_op jit(solution)/shard_map/ppermute | solution.py:19
  60.6 14.9 %copy-start.7 = (bf16[255,2048]{1,0:T(8,128)(2,1)}, bf16[255,2048]{1,0:T(8,128)(2,1)S(1)}, u32[]{:S(2)}) copy-start(bf16[255,2048]{1,0:T(8,128)(2,1)S(1)} %pad_maximum_fusion.1) | copy-start | bytes 3133444
  81.2 0.7 copy-start.16
  81.2 14.7 %copy-start.10 = (bf16[64,1024]{1,0:T(8,128)(2,1)S(1)}, bf16[64,1024]{1,0:T(8,128)(2,1)}, u32[]{:S(2)}) copy-start(bf16[64,1024]{1,0:T(8,128)(2,1)} %get-tuple-element.1836) | copy-start | bytes 393220
  81.2 15.0 %copy-start.14 = (bf16[128,128]{1,0:T(8,128)(2,1)S(1)}, bf16[128,128]{1,0:T(8,128)(2,1)}, u32[]{:S(2)}) copy-start(bf16[128,128]{1,0:T(8,128)(2,1)} %param.34) | copy-start | bytes 98308
  81.2 47.9 %copy-start.15 = (bf16[128,128]{1,0:T(8,128)(2,1)S(1)}, bf16[128,128]{1,0:T(8,128)(2,1)}, u32[]{:S(2)}) copy-start(bf16[128,128]{1,0:T(8,128)(2,1)} %param.35) | copy-start | bytes 98308
  81.2 179.4 %reduce-scatter.2.cloned.1.call-start = ((), (), s32[]{:S(2)}) async-start(), calls=%async_computation.2 | async-start | bytes 1179648 | tf_op jit(solution)/shard_map/reduce_scatter | solution.py:232
  197.2 1.0 copy-start
  199.8 16.6 %copy-start.8 = (bf16[255,2048]{1,0:T(8,128)(2,1)S(1)}, bf16[255,2048]{1,0:T(8,128)(2,1)}, u32[]{:S(2)}) copy-start(bf16[255,2048]{1,0:T(8,128)(2,1)} %copy-done.7) | copy-start | bytes 3133444
  216.5 11.5 %copy-start.5 = (bf16[128,2048]{1,0:T(8,128)(2,1)S(1)}, bf16[128,2048]{1,0:T(8,128)(2,1)}, u32[]{:S(2)}) copy-start(bf16[128,2048]{1,0:T(8,128)(2,1)} %param.32) | copy-start | bytes 1572868
Sparse Core Ops, SparseCore 0:
  81.3 78.4 all-reduce.1
  198.3 62.2 reduce-scatter.1
where the time goes:
time: 272 us; the launch traced here: 269 us
  blocking collectives  105 us (39%)
  matrix products  47.4 us (17%)
  waiting for transfers between devices  46.7 us (17%)
  local copies, waits for them, and re-layouts  29.5 us (11%)
  between operations  14.5 us (5%)
  loops' own time  11 us (4%)
  other arithmetic  9.31 us (3%)
  starting transfers between devices  5.44 us (2%)
    conv_general_dilated x3, matrix products, depthwise(): lax.conv_general_dilated(signal[None], kernel[:, None, :], (1,), ((0, 0),...  37.8 us
    all_gather x1, blocking collectives, on_device(): lax.all_gather(attention_keys, 'seq', axis=0, tiled=True)  32.9 us
    all_gather x1, blocking collectives, on_device(): lax.all_gather(attention_values, 'seq', axis=0, tiled=True)  31.3 us
    reduce_scatter x1, waiting for transfers between devices, on_device(): lax.psum_scatter(buffer_all, 'seq', scatter_dimension=0, tiled=True)  28.9 us
    ppermute x2, waiting for transfers between devices, shifted(): return lax.ppermute(block, axis, route)  17.7 us
    psum x1, blocking collectives, on_device(): grad_filters, grad_gain = lax.psum((part_filters, part_gain), 'seq')  15.1 us
    all_gather x1, blocking collectives, on_device(): lax.all_gather(doc_ids.astype(jnp.bfloat16), 'seq', axis=0, tiled=True)  14 us
    psum x1, blocking collectives, on_device(): squares = lax.psum(jnp.sum(signal_rows * signal_rows, axis=1), 'head')  5.93 us
  transfers between devices with their start and end apart: 4, of which 3 were waited for; matrix products, arithmetic and copies ran while one was open for 18% of the time, Pallas kernels for 0%

commit v1 on v0

v1 whole, which is shorter than its diff:
```python
import functools

import jax
import jax.numpy as jnp
import ml_dtypes
import numpy as np
from jax import lax
from jax.experimental import pallas as pl
from jax.experimental.pallas import tpu as pltpu
from jax.sharding import PartitionSpec as P

HEAD = 128
NORM_EPS = 1e-05
FLOOR = -1e30
CHUNK = 512
F32 = jnp.float32
BF16 = jnp.bfloat16
MESH = pl.DeviceIdType.MESH


def split_const(x):
    high = x.astype(ml_dtypes.bfloat16)
    low = (x - high.astype(np.float64)).astype(ml_dtypes.bfloat16)
    return high, low


def dft_tables(rows):
    size = 2 * rows
    freq = 2 * np.pi * (np.arange(rows) + 0.5) / size
    angle = freq[:, None] * np.arange(size)[None, :]
    forward = np.concatenate([np.cos(angle), -np.sin(angle)], 0)
    back = np.concatenate([np.cos(angle[:, :rows]), -np.sin(angle[:, :rows])], 0).T * (2.0 / size)
    near = split_const(forward[:, :rows])
    far = split_const(forward[:, rows:])
    inverse = split_const(back)
    return near + far + inverse


def split(x):
    high = x.astype(BF16)
    return high, (x - high.astype(F32)).astype(BF16)


def dot(a, b):
    return lax.dot_general(a, b, (((1,), (0,)), ((), ())), preferred_element_type=F32)


def dot_t(a, b):
    return lax.dot_general(a, b, (((1,), (1,)), ((), ())), preferred_element_type=F32)


def wide(x, times):
    return jnp.concatenate([x] * times, axis=1)


def kernel(
    n, nh, model, cg, rg, rh, w,
    res, kgate, qgate, gain, filt, cot, query, keys, values, dout, docs,
    dnh, dnl, dfh, dfl, eh, el,
    g_res, g_kg, g_qg, g_gain, g_filt, g_q, g_k, g_v,
    inner_s, inner_h, gated_s, gated_h, f_s, g_s, gs_s,
    kvd, qt, dt, qf, df, dq, sbuf, rbuf, rs_src, rs_dst, ag, sq, al,
    in_ss, in_rs, ga_ss, ga_rs, kv_ss, kv_rs, dk_ss, dk_rs, rs_ss, rs_rs, ag_ss, ag_rs,
    sq_ss, sq_rs, al_ss, al_rs,
):
    me = lax.axis_index("seq")
    hd = lax.axis_index("head")
    rows, channels = res.shape
    chunks = channels // CHUNK
    heads = query.shape[1] // HEAD
    scale = HEAD ** (-0.5)

    def cols(c):
        return pl.ds(pl.multiple_of(c * CHUNK, CHUNK), CHUNK)

    def remote(src, dst, ss, rs, seq, head):
        return pltpu.make_async_remote_copy(
            src_ref=src, dst_ref=dst, send_sem=ss, recv_sem=rs,
            device_id=(seq, head), device_id_type=MESH,
        )

    def each(count, body):
        def step(j, _):
            body(j)
            return 0
        lax.fori_loop(0, count, step, 0)

    def others(count, mine, body):
        def step(j):
            @pl.when(j != mine)
            def _():
                body(j)
        each(count, step)

    barrier = pltpu.get_barrier_semaphore()
    others(n, me, lambda j: pl.semaphore_signal(barrier, inc=1, device_id=(j, hd), device_id_type=MESH))
    others(nh, hd, lambda j: pl.semaphore_signal(barrier, inc=1, device_id=(me, j), device_id_type=MESH))

    kvd[me, 0:rows, :] = keys[...]
    kvd[me, rows : 2 * rows, :] = values[...]
    kvd[me, 2 * rows : 2 * rows + 16, :] = jnp.broadcast_to(docs[...].astype(F32), (16, rows)).astype(BF16)

    def square_step(i, acc):
        x = res[:, pl.ds(pl.multiple_of(i * 128, 128), 128)].astype(F32)
        return acc + x * x

    part = lax.fori_loop(0, channels // 128, square_step, jnp.zeros((rows, 128), F32))
    sq[hd] = jnp.broadcast_to(jnp.sum(part.T, axis=0, keepdims=True), (8, rows))

    pl.semaphore_wait(barrier, n - 1 + nh - 1)

    def sq_copy(slot, peer):
        return remote(sq.at[slot], sq.at[slot], sq_ss.at[peer], sq_rs.at[slot], me, peer)

    def al_copy(slot, peer):
        return remote(al.at[slot], al.at[slot], al_ss.at[peer], al_rs.at[slot], me, peer)

    def kv_copy(slot, peer):
        return remote(kvd.at[slot], kvd.at[slot], kv_ss.at[peer], kv_rs.at[slot], peer, hd)

    others(nh, hd, lambda j: sq_copy(hd, j).start())

    def send_kv(j):
        @pl.when(j > me)
        def _():
            kv_copy(me, j).start()
    each(n, send_kv)

    prev = jnp.maximum(me - 1, 0)
    succ = jnp.minimum(me + 1, n - 1)

    def in_copy(c):
        return remote(inner_s.at[c], inner_h.at[c], in_ss.at[c], in_rs.at[c], prev, hd)

    def ga_copy(c):
        return remote(gated_s.at[c], gated_h.at[c], ga_ss.at[c], ga_rs.at[c], succ, hd)

    def make_inner(c):
        inner_s[c] = (cot[:, cols(c)].astype(F32) * qgate[:, cols(c)].astype(F32)).astype(BF16)

        @pl.when(me > 0)
        def _():
            in_copy(c).start()
    each(chunks, make_inner)

    @pl.when(me == n - 1)
    def _():
        inner_h[...] = jnp.zeros_like(inner_h)

    @pl.when(me == 0)
    def _():
        gated_h[...] = jnp.zeros_like(gated_h)

    def filter_spectrum(c):
        block = filt[pl.ds(pl.multiple_of(c * CHUNK, CHUNK), CHUNK), :]
        fh, fl = split(block)
        f_s[c] = dot_t(dnh[...], fh) + (dot_t(dnh[...], fl) + dot_t(dnl[...], fh))
    each(chunks, filter_spectrum)

    others(nh, hd, lambda j: sq_copy(j, j).wait_recv())
    total = sq[0]
    for j in range(1, nh):
        total = total + sq[j]
    inv_row = lax.rsqrt(total * (1.0 / model) + NORM_EPS)
    inv = jnp.broadcast_to(inv_row[0:1, :], (128, rows)).T

    def norm_of(c):
        return res[:, cols(c)].astype(F32) * wide(inv, CHUNK // 128)

    def make_gated(c):
        scaled = norm_of(c) * gain[:, cols(c)]
        gated = (scaled * kgate[:, cols(c)].astype(F32)).astype(BF16)
        gated_s[c] = gated

        @pl.when(me < n - 1)
        def _():
            ga_copy(c).start()
        g_s[c] = dot(dnh[...], gated) + dot(dnl[...], gated)
    each(chunks, make_gated)

    for h in range(heads):
        span = slice(h * HEAD, (h + 1) * HEAD)
        span_rows = slice(h * rows, (h + 1) * rows)
        q = query[:, span]
        d = dout[:, span]
        qf[span_rows, :] = q
        df[span_rows, :] = d
        qt[:, span_rows] = q.astype(F32).T.astype(BF16)
        dt[:, span_rows] = d.astype(F32).T.astype(BF16)

    my_docs = jnp.broadcast_to(docs[...].astype(F32), (rows, rows))
    row_at = lax.broadcasted_iota(jnp.int32, (rows, rows), 0)
    col_at = lax.broadcasted_iota(jnp.int32, (rows, rows), 1)

    def scores_of(j):
        key_docs = jnp.broadcast_to(kvd[j, 2 * rows : 2 * rows + 16, :].astype(F32)[0:1, :], (rows, rows)).T
        allowed = (key_docs == my_docs) & ((row_at <= col_at) | (j < me))
        bias = jnp.where(allowed, 0.0, FLOOR)
        return dot(kvd[j, 0:rows, :], qt[...]) * scale + wide(bias, heads)

    def wait_kv(j):
        @pl.when(j < me)
        def _():
            kv_copy(j, j).wait_recv()

    def max_step(j, top):
        wait_kv(j)
        return jnp.maximum(top, jnp.max(scores_of(j), axis=0, keepdims=True))

    flat = heads * rows
    top = lax.fori_loop(0, me + 1, max_step, jnp.full((1, flat), FLOOR, F32))

    def sum_step(j, state):
        total_p, total_w = state
        p = jnp.exp(scores_of(j) - top)
        dp = dot(kvd[j, rows : 2 * rows, :], dt[...])
        return (
            total_p + jnp.sum(p, axis=0, keepdims=True),
            total_w + jnp.sum(p * dp, axis=0, keepdims=True),
        )

    zero = jnp.zeros((1, flat), F32)
    total_p, total_w = lax.fori_loop(0, me + 1, sum_step, (zero, zero))
    inv_p = 1.0 / total_p
    delta = total_w * inv_p

    dq[...] = jnp.zeros_like(dq)

    def dk_copy(peer, slot):
        return remote(sbuf.at[peer], rbuf.at[slot], dk_ss.at[peer], dk_rs.at[slot], peer, hd)

    def grad_step(j, acc):
        p = jnp.exp(scores_of(j) - top) * inv_p
        dp = dot(kvd[j, rows : 2 * rows, :], dt[...])
        ds = (p * (dp - delta)).astype(BF16)
        dv = dot(p.astype(BF16), df[...])
        dk = dot(ds, qf[...]) * scale
        key_t = kvd[j, 0:rows, :].astype(F32).T.astype(BF16)
        dq[...] += dot(key_t, ds)
        both = jnp.concatenate([dk, dv], axis=0)
        sbuf[j] = both.astype(BF16)

        @pl.when(j < me)
        def _():
            dk_copy(j, me).start()
        return both

    own = lax.fori_loop(0, me + 1, grad_step, jnp.zeros((2 * rows, HEAD), F32))
    for h in range(heads):
        g_q[:, h * HEAD : (h + 1) * HEAD] = (dq[:, h * rows : (h + 1) * rows].T * scale).astype(BF16)

    def synth(re, im):
        sh, sl = split(jnp.concatenate([re, im], axis=0))
        return dot(eh[...], sh) + (dot(eh[...], sl) + dot(el[...], sh))

    def back_step(c, acc):
        @pl.when(me < n - 1)
        def _():
            in_copy(c).wait_recv()
        mine = inner_s[c]
        far = inner_h[c]
        u = (dot(dnh[...], mine) + dot(dfh[...], far)) + (dot(dnl[...], mine) + dot(dfl[...], far))
        ur, ui = u[:rows], u[rows:]
        gr, gi = g_s[c, 0:rows, :], g_s[c, rows : 2 * rows, :]
        taps = synth(ur * gr + ui * gi, ui * gr - ur * gi)
        fr, fi = f_s[c, 0:rows, :], f_s[c, rows : 2 * rows, :]
        back = synth(ur * fr + ui * fi, ui * fr - ur * fi)
        normed = norm_of(c)
        weight = gain[:, cols(c)]
        g_kg[:, cols(c)] = (back * (normed * weight)).astype(BF16)
        gs = back * kgate[:, cols(c)].astype(F32)
        gs_s[c] = gs
        prod = gs * normed
        gain_row = jnp.sum(prod, axis=0, keepdims=True)
        full = jnp.concatenate([taps, jnp.broadcast_to(gain_row, (rg * rh - rows, CHUNK))], axis=0).astype(BF16)
        per = CHUNK // w
        for a in range(per):
            for r in range(rg):
                rs_src[r * cg + c * per + a] = full[r * rh : (r + 1) * rh, a * w : (a + 1) * w]
        prod = prod * weight
        for a in range(CHUNK // 128):
            acc = acc + prod[:, a * 128 : (a + 1) * 128]
        return acc

    along = lax.fori_loop(0, chunks, back_step, jnp.zeros((rows, 128), F32))
    al[hd] = jnp.broadcast_to(jnp.sum(along.T, axis=0, keepdims=True), (8, rows))
    others(nh, hd, lambda j: al_copy(hd, j).start())

    def rs_copy(peer, slot):
        return remote(rs_src.at[peer], rs_dst.at[slot], rs_ss.at[peer], rs_rs.at[slot], peer, hd)

    def ag_copy(slot, peer):
        return remote(ag.at[slot], ag.at[slot], ag_ss.at[peer], ag_rs.at[slot], peer, hd)

    others(n, me, lambda j: rs_copy(j, me).start())

    def query_gate_step(c):
        @pl.when(me > 0)
        def _():
            ga_copy(c).wait_recv()
        far = gated_h[c]
        wv = g_s[c] - (dot(dfh[...], far) + dot(dfl[...], far))
        wr, wi = wv[:rows], wv[rows:]
        fr, fi = f_s[c, 0:rows, :], f_s[c, rows : 2 * rows, :]
        filtered = synth(wr * fr - wi * fi, wr * fi + wi * fr)
        g_qg[:, cols(c)] = (cot[:, cols(c)].astype(F32) * filtered).astype(BF16)
    each(chunks, query_gate_step)

    def rs_step(j, acc):
        rs_copy(j, j).wait_recv()
        return acc + rs_dst[j].astype(F32)

    mine = rs_src[me].astype(F32)
    mine = lax.fori_loop(0, me, rs_step, mine)
    mine = lax.fori_loop(me + 1, n, rs_step, mine)
    ag[me] = mine.astype(BF16)
    others(n, me, lambda j: ag_copy(me, j).start())

    others(nh, hd, lambda j: al_copy(j, j).wait_recv())
    along_sum = al[0]
    for j in range(1, nh):
        along_sum = along_sum + al[j]
    along_col = jnp.broadcast_to(along_sum[0:1, :] * (1.0 / model), (128, rows)).T

    def res_step(c):
        times = CHUNK // 128
        out = gain[:, cols(c)] * gs_s[c] - norm_of(c) * wide(along_col, times)
        g_res[:, cols(c)] = (wide(inv, times) * out).astype(BF16)
    each(chunks, res_step)

    def dk_step(j, acc):
        dk_copy(j, j).wait_recv()
        return acc + rbuf[j].astype(F32)

    own = lax.fori_loop(me + 1, n, dk_step, own)
    g_k[...] = own[:rows].astype(BF16)
    g_v[...] = own[rows:].astype(BF16)

    others(n, me, lambda j: ag_copy(j, j).wait_recv())

    def out_step(g):
        full = jnp.concatenate([ag[r * cg + g].astype(F32) for r in range(rg)], axis=0)
        g_filt[pl.ds(pl.multiple_of(g * w, w), w), :] = full[:rows].T
        g_gain[:, pl.ds(pl.multiple_of(g * w, w), w)] = full[rows : rows + 1]
    each(cg, out_step)

    others(nh, hd, lambda j: sq_copy(hd, j).wait_send())
    others(nh, hd, lambda j: al_copy(hd, j).wait_send())

    def sent_kv(j):
        @pl.when(j > me)
        def _():
            kv_copy(me, j).wait_send()

        @pl.when(j < me)
        def _():
            dk_copy(j, me).wait_send()
    each(n, sent_kv)

    def sent_halo(c):
        @pl.when(me > 0)
        def _():
            in_copy(c).wait_send()

        @pl.when(me < n - 1)
        def _():
            ga_copy(c).wait_send()
    each(chunks, sent_halo)
    others(n, me, lambda j: rs_copy(j, me).wait_send())
    others(n, me, lambda j: ag_copy(me, j).wait_send())


def on_device(n, nh, *args):
    (res, kgate, qgate, gain, filt, cot, query, keys, values, dout, docs) = args
    rows, channels = res.shape
    heads = query.shape[1] // HEAD
    chunks = channels // CHUNK
    cg = min(n, channels // 128)
    rg = n // cg
    w = channels // cg
    rh = -(-(filt.shape[1] + 1) // (16 * rg)) * 16
    size = 2 * rows
    flat = heads * rows
    tables = [jnp.asarray(t) for t in dft_tables(rows)]
    vmem = pl.BlockSpec(memory_space=pltpu.VMEM)
    dma = pltpu.SemaphoreType.DMA
    outs = (
        jax.ShapeDtypeStruct(res.shape, BF16),
        jax.ShapeDtypeStruct(res.shape, BF16),
        jax.ShapeDtypeStruct(res.shape, BF16),
        jax.ShapeDtypeStruct((1, channels), F32),
        jax.ShapeDtypeStruct(filt.shape, F32),
        jax.ShapeDtypeStruct(query.shape, BF16),
        jax.ShapeDtypeStruct(keys.shape, BF16),
        jax.ShapeDtypeStruct(values.shape, BF16),
    )
    block = (chunks, rows, CHUNK)
    scratch = [
        pltpu.VMEM(block, BF16),
        pltpu.VMEM(block, BF16),
        pltpu.VMEM(block, BF16),
        pltpu.VMEM(block, BF16),
        pltpu.VMEM((chunks, size, CHUNK), F32),
        pltpu.VMEM((chunks, size, CHUNK), F32),
        pltpu.VMEM(block, F32),
        pltpu.VMEM((n, size + 16, HEAD), BF16),
        pltpu.VMEM((HEAD, flat), BF16),
        pltpu.VMEM((HEAD, flat), BF16),
        pltpu.VMEM((flat, HEAD), BF16),
        pltpu.VMEM((flat, HEAD), BF16),
        pltpu.VMEM((HEAD, flat), F32),
        pltpu.VMEM((n, size, HEAD), BF16),
        pltpu.VMEM((n, size, HEAD), BF16),
        pltpu.VMEM((n, rh, w), BF16),
        pltpu.VMEM((n, rh, w), BF16),
        pltpu.VMEM((n, rh, w), BF16),
        pltpu.VMEM((nh, 8, rows), F32),
        pltpu.VMEM((nh, 8, rows), F32),
    ]
    scratch += [dma((chunks,))] * 4 + [dma((n,))] * 8 + [dma((nh,))] * 4
    result = pl.pallas_call(
        functools.partial(kernel, n, nh, nh * channels, cg, rg, rh, w),
        out_shape=outs,
        in_specs=[vmem] * (11 + len(tables)),
        out_specs=(vmem,) * len(outs),
        scratch_shapes=scratch,
        compiler_params=pltpu.CompilerParams(
            collective_id=0, has_side_effects=True, vmem_limit_bytes=56 * 1024 * 1024
        ),
        name="hyena_attention_backward",
    )(
        res, kgate, qgate, gain.reshape(1, channels), filt, cot, query, keys, values, dout,
        docs.reshape(1, rows), *tables,
    )
    return result[:3] + (result[3].reshape(channels),) + result[4:]


def solution(mesh):
    n, nh = mesh.shape["seq"], mesh.shape["head"]
    rows = P("seq", "head")
    return jax.shard_map(
        functools.partial(on_device, n, nh),
        mesh=mesh,
        in_specs=(rows, rows, rows, P("head"), P("head", None), rows, rows, rows, rows, rows, P("seq")),
        out_specs=(rows, rows, rows, P("head"), P("head", None), rows, rows, rows),
        check_vma=False,
    )
```

time: 272 us -> 77.7 us (0.29)
  blocking collectives: 105 us -> 0 us
  Pallas kernels: 0 us -> 68.6 us
  matrix products: 47.4 us -> 0 us
  waiting for transfers between devices: 46.7 us -> 0 us
  local copies, waits for them, and re-layouts: 29.5 us -> 7.4 us
  between operations: 14.5 us -> 0.67 us
  loops' own time: 11 us -> 0 us
  other arithmetic: 9.31 us -> 0 us
  starting transfers between devices: 5.44 us -> 0 us
    all_gather x3 -> x0, blocking collectives: 78.2 us -> none  [the longest x1 32.9 us: on_device(): lax.all_gather(attention_keys, 'seq', axis=0, tiled=True)]
    pallas_call x0 -> x1, Pallas kernels: none -> 68.6 us  [on_device(): pl.pallas_call(functools.partial(kernel, n, nh, nh * channels, cg, rg, rh...]
    conv_general_dilated x3 -> x0, matrix products: 37.8 us -> none  [depthwise(): lax.conv_general_dilated(signal[None], kernel[:, None, :], (1,), ((0, 0),...]
    reduce_scatter x1 -> x0, waiting for transfers between devices: 28.9 us -> none  [on_device(): lax.psum_scatter(buffer_all, 'seq', scatter_dimension=0, tiled=True)]
    psum x3 -> x0, blocking collectives: 27 us -> none  [the longest x1 15.1 us: on_device(): grad_filters, grad_gain = lax.psum((part_filters, part_gain), 'seq')]
    ppermute x2 -> x0, waiting for transfers between devices: 17.7 us -> none  [shifted(): return lax.ppermute(block, axis, route)]
    another operation x12 -> x0, loops' own time: 11 us -> none  [the longest x2 5.38 us: full_sweep(): lax.fori_loop(0, total_rows // block_rows, full_advance, (jnp.zeros((flat...]
    dot_general x28 -> x0, matrix products: 9.66 us -> none  [the longest x4 1.69 us: group_update(): jnp.einsum('rd,kd->rk', cotangent_flat, value_blk, preferred_element_type...]
  transfers between devices with their start and end apart: 4 -> 0, of which waited for: 3 -> 0; matrix products, arithmetic and copies ran while one was open for 18% -> 0% of each run, Pallas kernels for 0% -> 0%
where the time goes in v1:
time: 77.7 us; the launch traced here: 76.7 us
  Pallas kernels  68.6 us (88%)
  local copies, waits for them, and re-layouts  7.4 us (10%)
    pallas_call x1, Pallas kernels, on_device(): pl.pallas_call(functools.partial(kernel, n, nh, nh * channels, cg, rg, rh...  68.6 us
    unnamed x22, local copies, waits for them, and re-layouts  7.4 us

profile of v1, /device:TPU:26, one launch (start us, length us, event | category | flops | bytes accessed | tf_op | source)
XLA Modules:
  0.0 76.7 jit_solution(15910793288072864606)
XLA Ops:
  0.6 68.6 %hyena_attention_backward.1 = (bf16[128,2048]{1,0:T(8,128)(2,1)}, bf16[128,2048]{1,0:T(8,128)(2,1)}, bf16[128,2048]{1,0:T(8,128)(2,1)}, f32[1,2048]{1,0:T(1,128)...) custom-call(bf16[128,2048]{1,0:T(8,128)(2,1)} %res.1, ...), custom_call_target="tpu_custom_call" | custom-call | tf_op jit(solution)/shard_map/hyena_attention_backward/pallas_call | solution.py:421
  69.2 0.0 copy-start.2
  69.3 0.0 copy-start.1
  69.3 2.0 %copy.33 = bf16[128,2048]{1,0:T(8,128)(2,1)} copy(bf16[128,2048]{1,0:T(8,128)(2,1)} %get-tuple-element.32) | data formatting | bytes 1048576
  71.2 0.0 copy-done.2
  71.2 0.0 copy-start
  71.2 0.8 %copy.34 = bf16[128,2048]{1,0:T(8,128)(2,1)} copy(bf16[128,2048]{1,0:T(8,128)(2,1)S(1)} %copy-done.2) | data formatting | bytes 1048576
  72.0 0.0 copy-done.1
  72.0 0.0 copy-start.6
  72.0 0.8 %copy.35 = bf16[128,2048]{1,0:T(8,128)(2,1)} copy(bf16[128,2048]{1,0:T(8,128)(2,1)S(1)} %copy-done.1) | data formatting | bytes 1048576
  72.8 0.0 copy-done.6
  72.8 0.6 copy.36
  73.4 0.0 copy-done
  73.4 0.0 copy-start.3
  73.4 1.0 %copy.37 = f32[2048,128]{1,0:T(8,128)} copy(f32[2048,128]{1,0:T(8,128)S(1)} %copy-done) | data formatting | bytes 2097152
  74.4 0.1 copy-done.3
  74.5 0.0 copy-start.5
  74.5 0.7 copy.38
  75.2 0.1 copy-done.5
  75.3 0.0 copy-start.4
  75.3 0.6 copy.39
  75.9 0.2 copy-done.4
  76.1 0.6 copy.40
Async XLA Ops:
  69.2 2.0 %copy-start.2 = (bf16[128,2048]{1,0:T(8,128)(2,1)S(1)}, bf16[128,2048]{1,0:T(8,128)(2,1)}, u32[]{:S(2)}) copy-start(bf16[128,2048]{1,0:T(8,128)(2,1)} %get-tuple-element.33) | copy-start | bytes 1572868
  69.3 2.8 %copy-start.1 = (bf16[128,2048]{1,0:T(8,128)(2,1)S(1)}, bf16[128,2048]{1,0:T(8,128)(2,1)}, u32[]{:S(2)}) copy-start(bf16[128,2048]{1,0:T(8,128)(2,1)} %get-tuple-element.34) | copy-start | bytes 1572868
  71.2 2.2 %copy-start = (f32[2048,128]{1,0:T(8,128)S(1)}, f32[2048,128]{1,0:T(8,128)}, u32[]{:S(2)}) copy-start(f32[2048,128]{1,0:T(8,128)} %get-tuple-element.36) | copy-start | bytes 3145732
  72.0 0.8 %copy-start.6 = (f32[1,2048]{1,0:T(1,128)S(1)}, f32[1,2048]{1,0:T(1,128)}, u32[]{:S(2)}) copy-start(f32[1,2048]{1,0:T(1,128)} %get-tuple-element.19) | copy-start | bytes 24580
  73.4 1.1 %copy-start.3 = (bf16[128,1024]{1,0:T(8,128)(2,1)S(1)}, bf16[128,1024]{1,0:T(8,128)(2,1)}, u32[]{:S(2)}) copy-start(bf16[128,1024]{1,0:T(8,128)(2,1)} %get-tuple-element.37) | copy-start | bytes 786436
  74.5 0.8 copy-start.5
  75.3 0.8 %copy-start.4 = (bf16[128,128]{1,0:T(8,128)(2,1)S(1)}, bf16[128,128]{1,0:T(8,128)(2,1)}, u32[]{:S(2)}) copy-start(bf16[128,128]{1,0:T(8,128)(2,1)} %get-tuple-element.39) | copy-start | bytes 98308

commit v2 on v1

--- a/solution.py
+++ b/solution.py
@@ -29,7 +29,8 @@
     freq = 2 * np.pi * (np.arange(rows) + 0.5) / size
     angle = freq[:, None] * np.arange(size)[None, :]
     forward = np.concatenate([np.cos(angle), -np.sin(angle)], 0)
-    back = np.concatenate([np.cos(angle[:, :rows]), -np.sin(angle[:, :rows])], 0).T * (2.0 / size)
+    wave = angle[:, :rows].T
+    back = np.concatenate([np.cos(wave), -np.sin(wave)], 0) * (2.0 / size)
     near = split_const(forward[:, :rows])
     far = split_const(forward[:, rows:])
     inverse = split_const(back)
@@ -54,14 +55,14 @@
 
 
 def kernel(
-    n, nh, model, cg, rg, rh, w,
+    n, nh, model, cg, rg, rh, w, ph,
     res, kgate, qgate, gain, filt, cot, query, keys, values, dout, docs,
     dnh, dnl, dfh, dfl, eh, el,
     g_res, g_kg, g_qg, g_gain, g_filt, g_q, g_k, g_v,
     inner_s, inner_h, gated_s, gated_h, f_s, g_s, gs_s,
-    kvd, qt, dt, qf, df, dq, sbuf, rbuf, rs_src, rs_dst, ag, sq, al,
-    in_ss, in_rs, ga_ss, ga_rs, kv_ss, kv_rs, dk_ss, dk_rs, rs_ss, rs_rs, ag_ss, ag_rs,
-    sq_ss, sq_rs, al_ss, al_rs,
+    kvd, qt, dt, qf, df, dq, sbuf, rbuf, rs_src, y_dst, z_src, rs_dst, ag, sq, al,
+    in_ss, in_rs, ga_ss, ga_rs, kv_ss, kv_rs, dk_ss, dk_rs, rs_ss, rs_rs, ag_ss, ag_rs, fb_ss, fb_rs,
+    y_ss, y_rs, sq_ss, sq_rs, al_ss, al_rs,
 ):
     me = lax.axis_index("seq")
     hd = lax.axis_index("head")
@@ -120,12 +121,6 @@
 
     others(nh, hd, lambda j: sq_copy(hd, j).start())
 
-    def send_kv(j):
-        @pl.when(j > me)
-        def _():
-            kv_copy(me, j).start()
-    each(n, send_kv)
-
     prev = jnp.maximum(me - 1, 0)
     succ = jnp.minimum(me + 1, n - 1)
 
@@ -142,6 +137,7 @@
         def _():
             in_copy(c).start()
     each(chunks, make_inner)
+
 
     @pl.when(me == n - 1)
     def _():
@@ -150,6 +146,12 @@
     @pl.when(me == 0)
     def _():
         gated_h[...] = jnp.zeros_like(gated_h)
+
+    def send_kv(j):
+        @pl.when(j > me)
+        def _():
+            kv_copy(me, j).start()
+    each(n, send_kv)
 
     def filter_spectrum(c):
         block = filt[pl.ds(pl.multiple_of(c * CHUNK, CHUNK), CHUNK), :]
@@ -171,87 +173,40 @@
         scaled = norm_of(c) * gain[:, cols(c)]
         gated = (scaled * kgate[:, cols(c)].astype(F32)).astype(BF16)
         gated_s[c] = gated
-
-        @pl.when(me < n - 1)
-        def _():
-            ga_copy(c).start()
         g_s[c] = dot(dnh[...], gated) + dot(dnl[...], gated)
     each(chunks, make_gated)
 
-    for h in range(heads):
-        span = slice(h * HEAD, (h + 1) * HEAD)
-        span_rows = slice(h * rows, (h + 1) * rows)
-        q = query[:, span]
-        d = dout[:, span]
-        qf[span_rows, :] = q
-        df[span_rows, :] = d
-        qt[:, span_rows] = q.astype(F32).T.astype(BF16)
-        dt[:, span_rows] = d.astype(F32).T.astype(BF16)
-
-    my_docs = jnp.broadcast_to(docs[...].astype(F32), (rows, rows))
-    row_at = lax.broadcasted_iota(jnp.int32, (rows, rows), 0)
-    col_at = lax.broadcasted_iota(jnp.int32, (rows, rows), 1)
-
-    def scores_of(j):
-        key_docs = jnp.broadcast_to(kvd[j, 2 * rows : 2 * rows + 16, :].astype(F32)[0:1, :], (rows, rows)).T
-        allowed = (key_docs == my_docs) & ((row_at <= col_at) | (j < me))
-        bias = jnp.where(allowed, 0.0, FLOOR)
-        return dot(kvd[j, 0:rows, :], qt[...]) * scale + wide(bias, heads)
-
-    def wait_kv(j):
-        @pl.when(j < me)
-        def _():
-            kv_copy(j, j).wait_recv()
-
-    def max_step(j, top):
-        wait_kv(j)
-        return jnp.maximum(top, jnp.max(scores_of(j), axis=0, keepdims=True))
-
-    flat = heads * rows
-    top = lax.fori_loop(0, me + 1, max_step, jnp.full((1, flat), FLOOR, F32))
-
-    def sum_step(j, state):
-        total_p, total_w = state
-        p = jnp.exp(scores_of(j) - top)
-        dp = dot(kvd[j, rows : 2 * rows, :], dt[...])
-        return (
-            total_p + jnp.sum(p, axis=0, keepdims=True),
-            total_w + jnp.sum(p * dp, axis=0, keepdims=True),
-        )
-
-    zero = jnp.zeros((1, flat), F32)
-    total_p, total_w = lax.fori_loop(0, me + 1, sum_step, (zero, zero))
-    inv_p = 1.0 / total_p
-    delta = total_w * inv_p
-
-    dq[...] = jnp.zeros_like(dq)
-
-    def dk_copy(peer, slot):
-        return remote(sbuf.at[peer], rbuf.at[slot], dk_ss.at[peer], dk_rs.at[slot], peer, hd)
-
-    def grad_step(j, acc):
-        p = jnp.exp(scores_of(j) - top) * inv_p
-        dp = dot(kvd[j, rows : 2 * rows, :], dt[...])
-        ds = (p * (dp - delta)).astype(BF16)
-        dv = dot(p.astype(BF16), df[...])
-        dk = dot(ds, qf[...]) * scale
-        key_t = kvd[j, 0:rows, :].astype(F32).T.astype(BF16)
-        dq[...] += dot(key_t, ds)
-        both = jnp.concatenate([dk, dv], axis=0)
-        sbuf[j] = both.astype(BF16)
-
-        @pl.when(j < me)
-        def _():
-            dk_copy(j, me).start()
-        return both
-
-    own = lax.fori_loop(0, me + 1, grad_step, jnp.zeros((2 * rows, HEAD), F32))
-    for h in range(heads):
-        g_q[:, h * HEAD : (h + 1) * HEAD] = (dq[:, h * rows : (h + 1) * rows].T * scale).astype(BF16)
+    par = lax.rem(me, 2)
+    quarter = me // 2
+    partner = me + 1 - 2 * par
+
+    def half_copy(c):
+        return remote(rs_src.at[1 - par, c], y_dst.at[c], y_ss.at[c], y_rs.at[c], partner, hd)
+
+    def rs_copy(c, i, slot):
+        m = c * ph + i
+        return remote(z_src.at[c, i], rs_dst.at[slot], rs_ss.at[m], rs_rs.at[slot], 2 * m + par, hd)
+
+    def ag_copy(slot, j):
+        return remote(ag.at[slot], ag.at[slot], ag_ss.at[j], ag_rs.at[slot], 2 * j + par, hd)
+
+    def fb_copy(slot):
+        return remote(ag.at[slot], ag.at[slot], fb_ss.at[slot], fb_rs.at[slot], partner, hd)
+
+    def merge(c):
+        half_copy(c).wait_recv()
+        z_src[c] = (rs_src[par, c].astype(F32) + y_dst[c].astype(F32)).astype(BF16)
+        for i in range(ph):
+            @pl.when(c * ph + i != quarter)
+            def _():
+                rs_copy(c, i, quarter).start()
+
+    inv_h = jnp.concatenate([eh[0:rows, :], eh[rows : 2 * rows, :]], axis=1)
+    inv_l = jnp.concatenate([el[0:rows, :], el[rows : 2 * rows, :]], axis=1)
 
     def synth(re, im):
         sh, sl = split(jnp.concatenate([re, im], axis=0))
-        return dot(eh[...], sh) + (dot(eh[...], sl) + dot(el[...], sh))
+        return dot(inv_h, sh) + (dot(inv_h, sl) + dot(inv_l, sh))
 
     def back_step(c, acc):
         @pl.when(me < n - 1)
@@ -276,7 +231,13 @@
         per = CHUNK // w
         for a in range(per):
             for r in range(rg):
-                rs_src[r * cg + c * per + a] = full[r * rh : (r + 1) * rh, a * w : (a + 1) * w]
+                at = a * rg + r
+                rs_src[at % 2, c, at // 2] = full[r * rh : (r + 1) * rh, a * w : (a + 1) * w]
+        half_copy(c).start()
+
+        @pl.when(c > 0)
+        def _():
+            merge(c - 1)
         prod = prod * weight
         for a in range(CHUNK // 128):
             acc = acc + prod[:, a * 128 : (a + 1) * 128]
@@ -286,13 +247,107 @@
     al[hd] = jnp.broadcast_to(jnp.sum(along.T, axis=0, keepdims=True), (8, rows))
     others(nh, hd, lambda j: al_copy(hd, j).start())
 
-    def rs_copy(peer, slot):
-        return remote(rs_src.at[peer], rs_dst.at[slot], rs_ss.at[peer], rs_rs.at[slot], peer, hd)
-
-    def ag_copy(slot, peer):
-        return remote(ag.at[slot], ag.at[slot], ag_ss.at[peer], ag_rs.at[slot], peer, hd)
-
-    others(n, me, lambda j: rs_copy(j, me).start())
+    merge(chunks - 1)
+
+    def send_gated(c):
+        @pl.when(me < n - 1)
+        def _():
+            ga_copy(c).start()
+    each(chunks, send_gated)
+
+    for h in range(heads):
+        span = slice(h * HEAD, (h + 1) * HEAD)
+        span_rows = slice(h * rows, (h + 1) * rows)
+        q = query[:, span]
+        d = dout[:, span]
+        qf[span_rows, :] = q
+        df[span_rows, :] = d
+        qt[:, span_rows] = q.astype(F32).T.astype(BF16)
+        dt[:, span_rows] = d.astype(F32).T.astype(BF16)
+
+    my_docs = jnp.broadcast_to(docs[...].astype(F32), (rows, rows))
+    row_at = lax.broadcasted_iota(jnp.int32, (rows, rows), 0)
+    col_at = lax.broadcasted_iota(jnp.int32, (rows, rows), 1)
+
+    def scores_of(j):
+        key_docs = jnp.broadcast_to(kvd[j, 2 * rows : 2 * rows + 16, :].astype(F32)[0:1, :], (rows, rows)).T
+        allowed = (key_docs == my_docs) & ((row_at <= col_at) | (j < me))
+        bias = jnp.where(allowed, 0.0, FLOOR)
+        return dot(kvd[j, 0:rows, :], qt[...]) * scale + wide(bias, heads)
+
+    def wait_kv(j):
+        @pl.when(j < me)
+        def _():
+            kv_copy(j, j).wait_recv()
+
+    def max_step(j, top):
+        wait_kv(j)
+        return jnp.maximum(top, jnp.max(scores_of(j), axis=0, keepdims=True))
+
+    flat = heads * rows
+    top = lax.fori_loop(0, me + 1, max_step, jnp.full((1, flat), FLOOR, F32))
+
+    def sum_step(j, state):
+        total_p, total_w = state
+        p = jnp.exp(scores_of(j) - top)
+        dp = dot(kvd[j, rows : 2 * rows, :], dt[...])
+        return (
+            total_p + jnp.sum(p, axis=0, keepdims=True),
+            total_w + jnp.sum(p * dp, axis=0, keepdims=True),
+        )
+
+    zero = jnp.zeros((1, flat), F32)
+    total_p, total_w = lax.fori_loop(0, me + 1, sum_step, (zero, zero))
+    inv_p = 1.0 / total_p
+    delta = total_w * inv_p
+
+    def rs_step(j, acc):
+        rs_copy(j // ph, lax.rem(j, ph), j).wait_recv()
+        return acc + rs_dst[j].astype(F32)
+
+    mine = z_src[quarter // ph, lax.rem(quarter, ph)].astype(F32)
+    mine = lax.fori_loop(0, quarter, rs_step, mine)
+    mine = lax.fori_loop(quarter + 1, n // 2, rs_step, mine)
+    ag[me] = mine.astype(BF16)
+    others(n // 2, quarter, lambda j: ag_copy(me, j).start())
+    fb_copy(me).start()
+
+    dq[...] = jnp.zeros_like(dq)
+
+    def dk_copy(peer, slot):
+        return remote(sbuf.at[peer], rbuf.at[slot], dk_ss.at[peer], dk_rs.at[slot], peer, hd)
+
+    def grad_step(j, acc):
+        p = jnp.exp(scores_of(j) - top) * inv_p
+        dp = dot(kvd[j, rows : 2 * rows, :], dt[...])
+        ds = (p * (dp - delta)).astype(BF16)
+        dv = dot(p.astype(BF16), df[...])
+        dk = dot(ds, qf[...]) * scale
+        key_t = kvd[j, 0:rows, :].astype(F32).T.astype(BF16)
+        dq[...] += dot(key_t, ds)
+        both = jnp.concatenate([dk, dv], axis=0)
+        sbuf[j] = both.astype(BF16)
+
+        @pl.when(j < me)
+        def _():
+            dk_copy(j, me).start()
+        return both
+
+    own = lax.fori_loop(0, me + 1, grad_step, jnp.zeros((2 * rows, HEAD), F32))
+    for h in range(heads):
+        g_q[:, h * HEAD : (h + 1) * HEAD] = (dq[:, h * rows : (h + 1) * rows].T * scale).astype(BF16)
+
+    others(nh, hd, lambda j: al_copy(j, j).wait_recv())
+    along_sum = al[0]
+    for j in range(1, nh):
+        along_sum = along_sum + al[j]
+    along_col = jnp.broadcast_to(along_sum[0:1, :] * (1.0 / model), (128, rows)).T
+
+    def res_step(c):
+        times = CHUNK // 128
+        out = gain[:, cols(c)] * gs_s[c] - norm_of(c) * wide(along_col, times)
+        g_res[:, cols(c)] = (wide(inv, times) * out).astype(BF16)
+    each(chunks, res_step)
 
     def query_gate_step(c):
         @pl.when(me > 0)
@@ -306,27 +361,11 @@
         g_qg[:, cols(c)] = (cot[:, cols(c)].astype(F32) * filtered).astype(BF16)
     each(chunks, query_gate_step)
 
-    def rs_step(j, acc):
-        rs_copy(j, j).wait_recv()
-        return acc + rs_dst[j].astype(F32)
-
-    mine = rs_src[me].astype(F32)
-    mine = lax.fori_loop(0, me, rs_step, mine)
-    mine = lax.fori_loop(me + 1, n, rs_step, mine)
-    ag[me] = mine.astype(BF16)
-    others(n, me, lambda j: ag_copy(me, j).start())
-
-    others(nh, hd, lambda j: al_copy(j, j).wait_recv())
-    along_sum = al[0]
-    for j in range(1, nh):
-        along_sum = along_sum + al[j]
-    along_col = jnp.broadcast_to(along_sum[0:1, :] * (1.0 / model), (128, rows)).T
-
-    def res_step(c):
-        times = CHUNK // 128
-        out = gain[:, cols(c)] * gs_s[c] - norm_of(c) * wide(along_col, times)
-        g_res[:, cols(c)] = (wide(inv, times) * out).astype(BF16)
-    each(chunks, res_step)
+    def forward(j):
+        slot = 2 * j + par
+        ag_copy(slot, j).wait_recv()
+        fb_copy(slot).start()
+    others(n // 2, quarter, forward)
 
     def dk_step(j, acc):
         dk_copy(j, j).wait_recv()
@@ -336,10 +375,10 @@
     g_k[...] = own[:rows].astype(BF16)
     g_v[...] = own[rows:].astype(BF16)
 
-    others(n, me, lambda j: ag_copy(j, j).wait_recv())
+    each(n // 2, lambda j: fb_copy(2 * j + 1 - par).wait_recv())
 
     def out_step(g):
-        full = jnp.concatenate([ag[r * cg + g].astype(F32) for r in range(rg)], axis=0)
+        full = jnp.concatenate([ag[g * rg + r].astype(F32) for r in range(rg)], axis=0)
         g_filt[pl.ds(pl.multiple_of(g * w, w), w), :] = full[:rows].T
         g_gain[:, pl.ds(pl.multiple_of(g * w, w), w)] = full[rows : rows + 1]
     each(cg, out_step)
@@ -366,8 +405,24 @@
         def _():
             ga_copy(c).wait_send()
     each(chunks, sent_halo)
-    others(n, me, lambda j: rs_copy(j, me).wait_send())
-    others(n, me, lambda j: ag_copy(me, j).wait_send())
+    each(chunks, lambda c: half_copy(c).wait_send())
+    others(n // 2, quarter, lambda m: rs_copy(m // ph, lax.rem(m, ph), quarter).wait_send())
+    others(n // 2, quarter, lambda j: ag_copy(me, j).wait_send())
+    each(n // 2, lambda j: fb_copy(2 * j + par).wait_send())
+
+
+def settle(count, *refs):
+    held = refs[2 * count : 3 * count]
+    into, out = refs[3 * count :]
+    first = [pltpu.make_async_copy(refs[i], held[i], into.at[i]) for i in range(count)]
+    second = [pltpu.make_async_copy(held[i], refs[count + i], out.at[i]) for i in range(count)]
+    for copy in first:
+        copy.start()
+    for i in range(count):
+        first[i].wait()
+        second[i].start()
+    for copy in second:
+        copy.wait()
 
 
 def on_device(n, nh, *args):
@@ -379,6 +434,7 @@
     rg = n // cg
     w = channels // cg
     rh = -(-(filt.shape[1] + 1) // (16 * rg)) * 16
+    ph = n // (2 * chunks)
     size = 2 * rows
     flat = heads * rows
     tables = [jnp.asarray(t) for t in dft_tables(rows)]
@@ -411,15 +467,17 @@
         pltpu.VMEM((HEAD, flat), F32),
         pltpu.VMEM((n, size, HEAD), BF16),
         pltpu.VMEM((n, size, HEAD), BF16),
-        pltpu.VMEM((n, rh, w), BF16),
-        pltpu.VMEM((n, rh, w), BF16),
+        pltpu.VMEM((2, chunks, ph, rh, w), BF16),
+        pltpu.VMEM((chunks, ph, rh, w), BF16),
+        pltpu.VMEM((chunks, ph, rh, w), BF16),
+        pltpu.VMEM((n // 2, rh, w), BF16),
         pltpu.VMEM((n, rh, w), BF16),
         pltpu.VMEM((nh, 8, rows), F32),
         pltpu.VMEM((nh, 8, rows), F32),
     ]
-    scratch += [dma((chunks,))] * 4 + [dma((n,))] * 8 + [dma((nh,))] * 4
+    scratch += [dma((chunks,))] * 4 + [dma((n,))] * 10 + [dma((chunks,))] * 2 + [dma((nh,))] * 4
     result = pl.pallas_call(
-        functools.partial(kernel, n, nh, nh * channels, cg, rg, rh, w),
+        functools.partial(kernel, n, nh, nh * channels, cg, rg, rh, w, ph),
         out_shape=outs,
         in_specs=[vmem] * (11 + len(tables)),
         out_specs=(vmem,) * len(outs),
@@ -432,6 +490,16 @@
         res, kgate, qgate, gain.reshape(1, channels), filt, cot, query, keys, values, dout,
         docs.reshape(1, rows), *tables,
     )
+    anywhere = pl.BlockSpec(memory_space=pl.ANY)
+    result = pl.pallas_call(
+        functools.partial(settle, len(outs)),
+        out_shape=outs,
+        in_specs=[anywhere] * len(outs),
+        out_specs=(anywhere,) * len(outs),
+        scratch_shapes=[pltpu.VMEM(o.shape, o.dtype) for o in outs] + [dma((len(outs),))] * 2,
+        compiler_params=pltpu.CompilerParams(vmem_limit_bytes=56 * 1024 * 1024),
+        name="settle_outputs",
+    )(*result)
     return result[:3] + (result[3].reshape(channels),) + result[4:]
 
 

time: 77.7 us -> 62.6 us (0.81)
  local copies, waits for them, and re-layouts: 7.4 us -> 0 us
  Pallas kernels: 68.6 us -> 61.7 us
    pallas_call x1, Pallas kernels: 68.6 us -> 58.8 us  [on_device(): pl.pallas_call(functools.partial(kernel, n, nh, nh * channels, cg, rg, rh...]
    unnamed x22 -> x0, local copies, waits for them, and re-layouts: 7.4 us -> none
    pallas_call x0 -> x1, Pallas kernels: none -> 2.92 us  [on_device(): pl.pallas_call(functools.partial(settle, len(outs)), out_shape=outs, in_s...]
where the time goes in v2:
time: 62.6 us; the launch traced here: 62.3 us
  Pallas kernels  61.7 us (99%)
  between operations  0.65 us (1%)
    pallas_call x1, Pallas kernels, on_device(): pl.pallas_call(functools.partial(kernel, n, nh, nh * channels, cg, rg, rh...  58.8 us
    pallas_call x1, Pallas kernels, on_device(): pl.pallas_call(functools.partial(settle, len(outs)), out_shape=outs, in_s...  2.92 us

profile of v2, /device:TPU:26, one launch (start us, length us, event | category | flops | bytes accessed | tf_op | source)
XLA Modules:
  0.0 62.3 jit_solution(1501593976535214415)
XLA Ops:
  0.6 58.8 %hyena_attention_backward.1 = (bf16[128,2048]{1,0:T(8,128)(2,1)}, bf16[128,2048]{1,0:T(8,128)(2,1)}, bf16[128,2048]{1,0:T(8,128)(2,1)}, f32[1,2048]{1,0:T(1,128)...) custom-call(bf16[128,2048]{1,0:T(8,128)(2,1)} %res.1, ...), custom_call_target="tpu_custom_call" | custom-call | tf_op jit(solution)/shard_map/hyena_attention_backward/pallas_call | solution.py:479
  59.4 2.9 %settle_outputs.1 = (bf16[128,2048]{1,0:T(8,128)(2,1)}, bf16[128,2048]{1,0:T(8,128)(2,1)}, bf16[128,2048]{1,0:T(8,128)(2,1)}, f32[1,2048]{1,0:T(1,128)}, f32[204...) custom-call(bf16[128,2048]{1,0:T(8,128)(2,1)} %get-tuple-element.24.refs_0_, ...), custom_call_target="tpu_custom_call" | custom-call | tf_op jit(solution)/shard_map/settle_outputs/pallas_call | solution.py:494

commit v3 on v2

--- a/solution.py
+++ b/solution.py
@@ -58,8 +58,9 @@
     n, nh, model, cg, rg, rh, w, ph,
     res, kgate, qgate, gain, filt, cot, query, keys, values, dout, docs,
     dnh, dnl, dfh, dfl, eh, el,
-    g_res, g_kg, g_qg, g_gain, g_filt, g_q, g_k, g_v,
-    inner_s, inner_h, gated_s, gated_h, f_s, g_s, gs_s,
+    o_res, o_kg, o_qg, g_gain, g_filt, o_q, g_k, g_v,
+    g_res, g_kg, g_qg, g_q, out_sem,
+    inner_s, inner_h, gated_s, gated_h, f_s, g_s, u_s, gs_s,
     kvd, qt, dt, qf, df, dq, sbuf, rbuf, rs_src, y_dst, z_src, rs_dst, ag, sq, al,
     in_ss, in_rs, ga_ss, ga_rs, kv_ss, kv_rs, dk_ss, dk_rs, rs_ss, rs_rs, ag_ss, ag_rs, fb_ss, fb_rs,
     y_ss, y_rs, sq_ss, sq_rs, al_ss, al_rs,
@@ -93,10 +94,36 @@
                 body(j)
         each(count, step)
 
+    def leave(i):
+        held = (g_res, g_kg, g_qg, g_q)[i]
+        out = (o_res, o_kg, o_qg, o_q)[i]
+        return pltpu.make_async_copy(held, out, out_sem.at[i])
+
     barrier = pltpu.get_barrier_semaphore()
     others(n, me, lambda j: pl.semaphore_signal(barrier, inc=1, device_id=(j, hd), device_id_type=MESH))
     others(nh, hd, lambda j: pl.semaphore_signal(barrier, inc=1, device_id=(me, j), device_id_type=MESH))
 
+    prev = jnp.maximum(me - 1, 0)
+    succ = jnp.minimum(me + 1, n - 1)
+
+    def in_copy(c):
+        return remote(inner_s.at[c], inner_h.at[c], in_ss.at[c], in_rs.at[c], prev, hd)
+
+    def ga_copy(c):
+        return remote(gated_s.at[c], gated_h.at[c], ga_ss.at[c], ga_rs.at[c], succ, hd)
+
+    def make_inner(c):
+        inner_s[c] = (cot[:, cols(c)].astype(F32) * qgate[:, cols(c)].astype(F32)).astype(BF16)
+    each(chunks, make_inner)
+
+    pl.semaphore_wait(barrier, n - 1 + nh - 1)
+
+    def send_inner(c):
+        @pl.when(me > 0)
+        def _():
+            in_copy(c).start()
+    each(chunks, send_inner)
+
     kvd[me, 0:rows, :] = keys[...]
     kvd[me, rows : 2 * rows, :] = values[...]
     kvd[me, 2 * rows : 2 * rows + 16, :] = jnp.broadcast_to(docs[...].astype(F32), (16, rows)).astype(BF16)
@@ -108,8 +135,6 @@
     part = lax.fori_loop(0, channels // 128, square_step, jnp.zeros((rows, 128), F32))
     sq[hd] = jnp.broadcast_to(jnp.sum(part.T, axis=0, keepdims=True), (8, rows))
 
-    pl.semaphore_wait(barrier, n - 1 + nh - 1)
-
     def sq_copy(slot, peer):
         return remote(sq.at[slot], sq.at[slot], sq_ss.at[peer], sq_rs.at[slot], me, peer)
 
@@ -120,24 +145,6 @@
         return remote(kvd.at[slot], kvd.at[slot], kv_ss.at[peer], kv_rs.at[slot], peer, hd)
 
     others(nh, hd, lambda j: sq_copy(hd, j).start())
-
-    prev = jnp.maximum(me - 1, 0)
-    succ = jnp.minimum(me + 1, n - 1)
-
-    def in_copy(c):
-        return remote(inner_s.at[c], inner_h.at[c], in_ss.at[c], in_rs.at[c], prev, hd)
-
-    def ga_copy(c):
-        return remote(gated_s.at[c], gated_h.at[c], ga_ss.at[c], ga_rs.at[c], succ, hd)
-
-    def make_inner(c):
-        inner_s[c] = (cot[:, cols(c)].astype(F32) * qgate[:, cols(c)].astype(F32)).astype(BF16)
-
-        @pl.when(me > 0)
-        def _():
-            in_copy(c).start()
-    each(chunks, make_inner)
-
 
     @pl.when(me == n - 1)
     def _():
@@ -156,6 +163,7 @@
     def filter_spectrum(c):
         block = filt[pl.ds(pl.multiple_of(c * CHUNK, CHUNK), CHUNK), :]
         fh, fl = split(block)
+        u_s[c] = dot(dnh[...], inner_s[c]) + dot(dnl[...], inner_s[c])
         f_s[c] = dot_t(dnh[...], fh) + (dot_t(dnh[...], fl) + dot_t(dnl[...], fh))
     each(chunks, filter_spectrum)
 
@@ -212,9 +220,8 @@
         @pl.when(me < n - 1)
         def _():
             in_copy(c).wait_recv()
-        mine = inner_s[c]
         far = inner_h[c]
-        u = (dot(dnh[...], mine) + dot(dfh[...], far)) + (dot(dnl[...], mine) + dot(dfl[...], far))
+        u = u_s[c] + (dot(dfh[...], far) + dot(dfl[...], far))
         ur, ui = u[:rows], u[rows:]
         gr, gi = g_s[c, 0:rows, :], g_s[c, rows : 2 * rows, :]
         taps = synth(ur * gr + ui * gi, ui * gr - ur * gi)
@@ -248,6 +255,7 @@
     others(nh, hd, lambda j: al_copy(hd, j).start())
 
     merge(chunks - 1)
+    leave(1).start()
 
     def send_gated(c):
         @pl.when(me < n - 1)
@@ -337,6 +345,14 @@
     for h in range(heads):
         g_q[:, h * HEAD : (h + 1) * HEAD] = (dq[:, h * rows : (h + 1) * rows].T * scale).astype(BF16)
 
+    def forward(j):
+        slot = 2 * j + par
+        ag_copy(slot, j).wait_recv()
+        fb_copy(slot).start()
+    others(n // 2, quarter, forward)
+
+    leave(3).start()
+
     others(nh, hd, lambda j: al_copy(j, j).wait_recv())
     along_sum = al[0]
     for j in range(1, nh):
@@ -348,6 +364,7 @@
         out = gain[:, cols(c)] * gs_s[c] - norm_of(c) * wide(along_col, times)
         g_res[:, cols(c)] = (wide(inv, times) * out).astype(BF16)
     each(chunks, res_step)
+    leave(0).start()
 
     def query_gate_step(c):
         @pl.when(me > 0)
@@ -360,12 +377,7 @@
         filtered = synth(wr * fr - wi * fi, wr * fi + wi * fr)
         g_qg[:, cols(c)] = (cot[:, cols(c)].astype(F32) * filtered).astype(BF16)
     each(chunks, query_gate_step)
-
-    def forward(j):
-        slot = 2 * j + par
-        ag_copy(slot, j).wait_recv()
-        fb_copy(slot).start()
-    others(n // 2, quarter, forward)
+    leave(2).start()
 
     def dk_step(j, acc):
         dk_copy(j, j).wait_recv()
@@ -383,6 +395,8 @@
         g_gain[:, pl.ds(pl.multiple_of(g * w, w), w)] = full[rows : rows + 1]
     each(cg, out_step)
 
+    for i in range(4):
+        leave(i).wait()
     others(nh, hd, lambda j: sq_copy(hd, j).wait_send())
     others(nh, hd, lambda j: al_copy(hd, j).wait_send())
 
@@ -439,6 +453,7 @@
     flat = heads * rows
     tables = [jnp.asarray(t) for t in dft_tables(rows)]
     vmem = pl.BlockSpec(memory_space=pltpu.VMEM)
+    anywhere = pl.BlockSpec(memory_space=pl.ANY)
     dma = pltpu.SemaphoreType.DMA
     outs = (
         jax.ShapeDtypeStruct(res.shape, BF16),
@@ -452,10 +467,16 @@
     )
     block = (chunks, rows, CHUNK)
     scratch = [
+        pltpu.VMEM(res.shape, BF16),
+        pltpu.VMEM(res.shape, BF16),
+        pltpu.VMEM(res.shape, BF16),
+        pltpu.VMEM(query.shape, BF16),
+        dma((4,)),
         pltpu.VMEM(block, BF16),
         pltpu.VMEM(block, BF16),
         pltpu.VMEM(block, BF16),
         pltpu.VMEM(block, BF16),
+        pltpu.VMEM((chunks, size, CHUNK), F32),
         pltpu.VMEM((chunks, size, CHUNK), F32),
         pltpu.VMEM((chunks, size, CHUNK), F32),
         pltpu.VMEM(block, F32),
@@ -480,7 +501,7 @@
         functools.partial(kernel, n, nh, nh * channels, cg, rg, rh, w, ph),
         out_shape=outs,
         in_specs=[vmem] * (11 + len(tables)),
-        out_specs=(vmem,) * len(outs),
+        out_specs=(anywhere,) * 3 + (vmem,) * 2 + (anywhere,) + (vmem,) * 2,
         scratch_shapes=scratch,
         compiler_params=pltpu.CompilerParams(
             collective_id=0, has_side_effects=True, vmem_limit_bytes=56 * 1024 * 1024
@@ -490,7 +511,6 @@
         res, kgate, qgate, gain.reshape(1, channels), filt, cot, query, keys, values, dout,
         docs.reshape(1, rows), *tables,
     )
-    anywhere = pl.BlockSpec(memory_space=pl.ANY)
     result = pl.pallas_call(
         functools.partial(settle, len(outs)),
         out_shape=outs,

time: 62.6 us -> 61.7 us (0.986)
  Pallas kernels: 61.7 us -> 60.9 us
    pallas_call x1, Pallas kernels: 58.8 us -> 58 us  [on_device(): pl.pallas_call(functools.partial(kernel, n, nh, nh * channels, cg, rg, rh...]
where the time goes in v3:
time: 61.7 us; the launch traced here: 61.5 us
  Pallas kernels  60.9 us (99%)
  between operations  0.65 us (1%)
    pallas_call x1, Pallas kernels, on_device(): pl.pallas_call(functools.partial(kernel, n, nh, nh * channels, cg, rg, rh...  58 us
    pallas_call x1, Pallas kernels, on_device(): pl.pallas_call(functools.partial(settle, len(outs)), out_shape=outs, in_s...  2.92 us

profile of v3, /device:TPU:26, one launch (start us, length us, event | category | flops | bytes accessed | tf_op | source)
XLA Modules:
  0.0 61.5 jit_solution(16330436331274878621)
XLA Ops:
  0.6 58.0 %hyena_attention_backward.1 = (bf16[128,2048]{1,0:T(8,128)(2,1)}, bf16[128,2048]{1,0:T(8,128)(2,1)}, bf16[128,2048]{1,0:T(8,128)(2,1)}, f32[1,2048]{1,0:T(1,128)...) custom-call(bf16[128,2048]{1,0:T(8,128)(2,1)} %res.1, ...), custom_call_target="tpu_custom_call" | custom-call | tf_op jit(solution)/shard_map/hyena_attention_backward/pallas_call | solution.py:500
  58.6 2.9 %settle_outputs.1 = (bf16[128,2048]{1,0:T(8,128)(2,1)}, bf16[128,2048]{1,0:T(8,128)(2,1)}, bf16[128,2048]{1,0:T(8,128)(2,1)}, f32[1,2048]{1,0:T(1,128)}, f32[204...) custom-call(bf16[128,2048]{1,0:T(8,128)(2,1)} %get-tuple-element.24.refs_0_, ...), custom_call_target="tpu_custom_call" | custom-call | tf_op jit(solution)/shard_map/settle_outputs/pallas_call | solution.py:514
